TPU v7x, 32 devices: a whole 2x2x4 slice. The times are simulated.
32 devices in a mesh: loc: 8 (over y, x, core), tm: 4 (over z).
Axes of the slice: x: 2, y: 2, z: 4, core: 2. Of those that a mesh axis runs over, the one named last changes fastest.
Arguments:
- observed: float32 [1024, 512], P('loc', 'tm'), may hold values from -6 to 6
- observed_mask: int32 [1024, 512], P('loc', 'tm'), may hold values 0 or 1
- training_site_positions: float32 [2, 1024], replicated, may hold values from 0 to 1
- time_stamps: float32 [512], replicated, may hold values from 0 to 1
- noise_var: float32 [512], P('tm'), may hold values from 0.2 to 2
- test_coords: float32 [2, 1024], replicated, may hold values from 0 to 1
- site_order: int32 [1024], replicated, may hold values from 0 to 1023, each once
Outputs:
- solver_estimate: float32 [1024, 512], P('loc', 'tm')
- posterior_mean_field: float32 [1024, 512], P('loc', 'tm')
Inputs may be any that keep to these rules, and one draw needn't show every extreme that they name: `site_order`: each test site appears once.
All inputs are finite; a program needn't handle non-finite values. No bound on the sum of `observed_mask` on one device may be relied on, other than what follows from the above.
Results may differ from a plain program's by a relative error of at most 0.00022.
Values sent between devices are 32-bit elements; how exact they have to be, the bound alone decides.
A program may use at most 64 MiB of HBM per device.

v0:
```python
import math

import jax
import jax.numpy as jnp
from jax import lax
from jax.sharding import PartitionSpec as P

ITERS = 2


root_three = math.sqrt(3.0)
space_reach = 2.5
time_reach = 5.0
covariance_times_iterate = 0.1


def matern(left_points, right_points, length):
    squared = jnp.sum(jnp.square(left_points[:, :, None] - right_points[:, None, :]), axis=0)
    scaled = jnp.sqrt(squared) * (root_three / length)
    return (1.0 + scaled) * jnp.exp(-scaled)


def between_covariance_block(row_points, col_points, right_side, length):
    row_count = row_points.shape[1]
    block_size = math.gcd(row_count, 2048)
    number = row_count // block_size
    blocks = row_points.reshape(row_points.shape[0], number, block_size).transpose(1, 0, 2)

    def one_block(points):
        return jnp.dot(
            matern(points, col_points, length),
            right_side,
            precision=lax.Precision.HIGHEST,
            preferred_element_type=jnp.float32,
        )

    return lax.map(one_block, blocks).reshape(row_count, right_side.shape[1])


def column_sum(row_points, col_points, right_side, length):
    col_count = col_points.shape[1]
    block_size = math.gcd(col_count, 2048)
    number = col_count // block_size

    def add_block(index, summed):
        offset = index * block_size
        columns = lax.dynamic_slice_in_dim(col_points, offset, block_size, 1)
        rows_part = lax.dynamic_slice_in_dim(right_side, offset, block_size, 0)
        kernel = matern(row_points, columns, length)
        return summed + jnp.dot(
            kernel, rows_part, precision=lax.Precision.HIGHEST, preferred_element_type=jnp.float32
        )

    empty = jnp.zeros((row_points.shape[1], right_side.shape[1]), jnp.float32)
    return lax.fori_loop(0, number, add_block, empty)


def on_device(
    observed,
    observed_mask,
    training_site_positions,
    time_stamps,
    noise_var,
    test_coords,
    site_order,
):
    loc_rows = observed.shape[0]
    time_cols = observed.shape[1]
    mask_float = observed_mask.astype(jnp.float32)
    planar_correlation_range = space_reach / math.sqrt(training_site_positions.shape[1])
    time_length = time_reach / time_stamps.shape[0]
    own_points = lax.dynamic_slice_in_dim(
        training_site_positions, lax.axis_index("loc") * loc_rows, loc_rows, 1
    )
    own_stamps = lax.dynamic_slice_in_dim(
        time_stamps, lax.axis_index("tm") * time_cols, time_cols, 0
    )

    def time_fold(shard_piece):
        kernel = matern(time_stamps[None, :], own_stamps[None, :], time_length)
        return jnp.dot(
            shard_piece, kernel, precision=lax.Precision.HIGHEST, preferred_element_type=jnp.float32
        )

    def squares(residual):
        return lax.psum(jnp.sum(residual * residual), ("loc", "tm"))

    solver_estimate = jnp.zeros_like(observed)
    residual = mask_float * observed
    direction = residual
    norm_now = squares(residual)
    for iteration in range(ITERS):
        masked = mask_float * direction
        inner = time_fold(lax.all_gather(masked, "tm", axis=1, tiled=True))
        outer = column_sum(
            own_points,
            training_site_positions,
            lax.all_gather(inner, "loc", axis=0, tiled=True),
            planar_correlation_range,
        )
        image = mask_float * outer * covariance_times_iterate + direction * noise_var[None, :]
        curvature_sum = lax.psum(jnp.sum(direction * image), ("loc", "tm"))
        step_size = norm_now / curvature_sum
        solver_estimate = solver_estimate + step_size * direction
        residual = residual - step_size * image
        if iteration + 1 < ITERS:
            norm_next = squares(residual)
            direction = residual + norm_next / norm_now * direction
            norm_now = norm_next
    temporal_observation_grid = time_fold(lax.all_gather(solver_estimate, "tm", axis=1, tiled=True))
    unseen_site_positions = test_coords[:, site_order]
    local_share = lax.psum_scatter(
        between_covariance_block(
            unseen_site_positions, own_points, temporal_observation_grid, planar_correlation_range
        ),
        "loc",
        scatter_dimension=0,
        tiled=True,
    )
    posterior_mean_field = local_share * covariance_times_iterate
    return (solver_estimate, posterior_mean_field)


def solution(mesh):
    in_specs = (P("loc", "tm"), P("loc", "tm"), P(), P(), P("tm"), P(), P())
    out_specs = (P("loc", "tm"), P("loc", "tm"))
    return jax.shard_map(
        on_device, mesh=mesh, in_specs=in_specs, out_specs=out_specs, check_vma=False
    )
```

profile of v0, /device:TPU:0, one launch (start us, length us, event | category | flops | bytes accessed | tf_op | source)
XLA Modules:
  0.0 252.4 jit_solution(4973093367404506720)
XLA Ops:
  7.2 0.9 convert_multiply_fusion.1
  8.1 15.6 %all_gather.15 = f32[128,512]{1,0:T(8,128)S(1)} all-gather(f32[128,128]{1,0:T(8,128)S(1)} %get-tuple-element.41), channel_id=1, replica_groups=mesh['loc'=8,'tm'=4] {'tm'}, dimensions={1}, use_global_device_ids=true | all-gather | bytes 327680 | tf_op jit(solution)/shard_map/all_gather | solution.py:94
  23.7 0.7 copy-done.6
  24.5 0.6 fusion.17
  25.1 9.9 %all_gather.16 = f32[1024,128]{1,0:T(8,128)S(1)} all-gather(f32[128,128]{1,0:T(8,128)S(1)} %fusion.17), channel_id=1, replica_groups=mesh['loc'=8,'tm'=4] {'loc'}, dimensions={0}, use_global_device_ids=true | all-gather | bytes 589824 | tf_op jit(solution)/shard_map/all_gather | solution.py:98
  35.0 0.7 copy-done.2
  35.8 0.7 copy-done
  36.5 1.5 multiply_reduce_fusion.3
  38.0 40.0 %all-reduce = (f32[]{:T(128)}, f32[]{:T(128)}) all-reduce(f32[]{:T(128)} %get-tuple-element.38, f32[]{:T(128)} %get-tuple-element.37), channel_id=1, replica_groups=mesh['loc'=8,'tm'=4] {'loc','tm'}, use_global_device_ids=true, to_apply=%region_1.0 | all-reduce | flops 2 | bytes 16 | tf_op jit(solution)/shard_map/psum | solution.py:86
  79.3 0.6 multiply_reduce_fusion.2
  79.9 41.5 %psum.30 = f32[]{:T(128)} all-reduce(f32[]{:T(128)} %multiply_reduce_fusion.2), channel_id=1, replica_groups=mesh['loc'=8,'tm'=4] {'loc','tm'}, use_global_device_ids=true, to_apply=%region_6.0 | all-reduce | flops 1 | bytes 8 | tf_op jit(solution)/shard_map/psum | solution.py:86
  122.7 14.1 %all_gather.17 = f32[128,512]{1,0:T(8,128)S(1)} all-gather(f32[128,128]{1,0:T(8,128)S(1)} %convert_multiply_fusion), channel_id=1, replica_groups=mesh['loc'=8,'tm'=4] {'tm'}, dimensions={1}, use_global_device_ids=true | all-gather | bytes 327680 | tf_op jit(solution)/shard_map/all_gather | solution.py:94
  136.9 0.6 fusion.16
  137.5 11.0 %all_gather.18 = f32[1024,128]{1,0:T(8,128)S(1)} all-gather(f32[128,128]{1,0:T(8,128)S(1)} %fusion.16), channel_id=1, replica_groups=mesh['loc'=8,'tm'=4] {'loc'}, dimensions={0}, use_global_device_ids=true | all-gather | bytes 589824 | tf_op jit(solution)/shard_map/all_gather | solution.py:98
  148.4 1.5 fusion.5
  149.9 38.0 %psum.31 = f32[]{:T(128)} all-reduce(f32[]{:T(128)} %fusion.5), channel_id=1, replica_groups=mesh['loc'=8,'tm'=4] {'loc','tm'}, use_global_device_ids=true, to_apply=%region_8.0 | all-reduce | flops 1 | bytes 8 | tf_op jit(solution)/shard_map/psum | solution.py:102
  189.3 14.6 %all_gather.19 = f32[128,512]{1,0:T(8,128)S(1)} all-gather(f32[128,128]{1,0:T(8,128)S(1)} %multiply_add_fusion), channel_id=1, replica_groups=mesh['loc'=8,'tm'=4] {'tm'}, dimensions={1}, use_global_device_ids=true | all-gather | bytes 327680 | tf_op jit(solution)/shard_map/all_gather | solution.py:110
  203.9 0.6 fusion.15
  204.9 0.5 copy-done.4
  205.3 2.8 %gather_fusion = f32[1024,2]{1,0:T(8,128)S(1)} fusion(f32[2,1024]{0,1:T(8,128)S(1)} %copy.11, s32[1024]{0:T(1024)S(1)} %fusion.34), kind=kCustom, calls=%fused_computation | custom fusion | bytes 20480 | tf_op jit(solution)/shard_map/gather | solution.py:111
  208.3 0.4 multiply_reduce_fusion
  208.7 1.5 fusion.6
  210.2 33.9 %reduce-scatter.2.cloned.1.call-done = f32[128,128]{1,0:T(8,128)} async-done(((f32[1024,128]{1,0:T(8,128)}), f32[128,128]{1,0:T(8,128)}) %reduce-scatter.2.cloned.1.call-update) | async-done | bytes 65552 | tf_op jit(solution)/shard_map/reduce_scatter | solution.py:112
  244.1 1.5 broadcast_multiply_fusion
  (20 shorter events, 0.9 us)
Async XLA Ops:
  7.2 236.9 %reduce-scatter.2.cloned.1.call-start = ((), (), s32[]{:S(2)}) async-start(), calls=%async_computation.1 | async-start | bytes 589824 | tf_op jit(solution)/shard_map/reduce_scatter | solution.py:112
  23.7 0.7 copy-start.6
  35.0 0.7 copy-start.2
  35.6 0.8 copy-start
  35.8 0.7 copy-start.5
  189.3 14.6 %copy-start.1 = (f32[128,128]{1,0:T(8,128)}, f32[128,128]{1,0:T(8,128)S(1)}, u32[]{:S(2)}) copy-start(f32[128,128]{1,0:T(8,128)S(1)} %multiply_add_fusion) | copy-start | bytes 196612
  203.9 0.7 copy-start.3
  204.6 0.7 copy-start.4
Sparse Core Ops, SparseCore 0:
  210.3 33.6 reduce-scatter.1
where the time goes:
time: 253 us; the launch traced here: 252 us
  blocking collectives  185 us (73%)
  waiting for transfers between devices  33.9 us (13%)
  between operations  18.1 us (7%)
  matrix products  6.23 us (2%)
  local copies, waits for them, and re-layouts  5.9 us (2%)
  other arithmetic  3.53 us (1%)
    psum x2, blocking collectives, squares(): return lax.psum(jnp.sum(residual * residual), ('loc', 'tm'))  81.4 us
    psum x1, blocking collectives, on_device(): curvature_sum = lax.psum(jnp.sum(direction * image), ('loc', 'tm'))  38 us
    reduce_scatter x1, waiting for transfers between devices, on_device(): lax.psum_scatter(between_covariance_block(unseen_site_positions, own_poin...  33.9 us
    all_gather x2, blocking collectives, on_device(): inner = time_fold(lax.all_gather(masked, 'tm', axis=1, tiled=True))  29.8 us
    all_gather x2, blocking collectives, on_device(): lax.all_gather(inner, 'loc', axis=0, tiled=True)  20.8 us
    all_gather x1, blocking collectives, on_device(): lax.all_gather(solver_estimate, 'tm', axis=1, tiled=True)  14.6 us
  transfers between devices with their start and end apart: 1, of which 1 were waited for; matrix products, arithmetic and copies ran while one was open for 0% of the time, Pallas kernels for 0%

commit v1 on v0

v1 whole, which is shorter than its diff:
```python
import functools
import math

import jax
import jax.numpy as jnp
from jax import lax
from jax.experimental import pallas as pl
from jax.experimental.pallas import tpu as pltpu
from jax.sharding import PartitionSpec as P

MESH = pl.DeviceIdType.MESH
F32 = jnp.float32
BF16 = jnp.bfloat16

root_three = math.sqrt(3.0)
space_reach = 2.5
time_reach = 5.0
amplitude = 0.1
SCALARS = 8


def split(x):
    high = x.astype(BF16)
    return high, (x - high.astype(F32)).astype(BF16)


def dot(a, b):
    return jnp.dot(a, b, preferred_element_type=F32)


def dot3(a_high, a_low, b_high, b_low):
    return dot(a_high, b_high) + (dot(a_high, b_low) + dot(a_low, b_high))


def column_of(row, width):
    return jnp.transpose(jnp.broadcast_to(row, (width, row.shape[1])))


def matern_of(distance, length):
    scaled = distance * (root_three / length)
    return (1.0 + scaled) * jnp.exp(-scaled)


def lane_sums(*arrays):
    sums = [jnp.sum(a, axis=0, keepdims=True) for a in arrays]
    sums.append(jnp.zeros((SCALARS - len(sums), sums[0].shape[1]), F32))
    return jnp.concatenate(sums, axis=0)


def kernel(
    n_loc, n_tm,
    obs, mask, pos, stamps, noise, test, order,
    est, post,
    held, inner, red_t, red_l, ks, kx, kt,
    held_send, held_recv, inner_send, inner_recv, pass_send,
    rt_send, rt_recv, rl_send, rl_recv,
):
    loc, tm = lax.axis_index("loc"), lax.axis_index("tm")
    rows, cols = obs.shape
    n_chip = n_loc // 2
    chip, core = loc // 2, lax.rem(loc, 2)
    sibling = chip * 2 + (1 - core)
    space_length = space_reach / math.sqrt(pos.shape[1])
    time_length = time_reach / stamps.shape[1]
    tm_peers = [lax.rem(tm + d, n_tm) for d in range(1, n_tm)]
    loc_peers = [lax.rem(loc + d, n_loc) for d in range(1, n_loc)]
    mates = [lax.rem(chip + d, n_chip) * 2 + core for d in range(1, n_chip)]
    started = []

    barrier = pltpu.get_barrier_semaphore()
    for peer in tm_peers:
        pl.semaphore_signal(barrier, inc=1, device_id={"tm": peer}, device_id_type=MESH)
    for peer in loc_peers:
        pl.semaphore_signal(barrier, inc=1, device_id={"loc": peer}, device_id_type=MESH)

    def send(ref, slot, send_sem, recv_sems, where):
        copy = pltpu.make_async_remote_copy(
            src_ref=ref.at[slot],
            dst_ref=ref.at[slot],
            send_sem=send_sem,
            recv_sem=recv_sems.at[slot],
            device_id=where,
            device_id_type=MESH,
        )
        copy.start()
        started.append(copy)

    def arrived(ref, slot, recv_sems, send_sem):
        pltpu.make_async_remote_copy(
            src_ref=ref.at[slot],
            dst_ref=ref.at[slot],
            send_sem=send_sem,
            recv_sem=recv_sems.at[slot],
            device_id={"loc": sibling},
            device_id_type=MESH,
        ).wait_recv()

    def lanes(index, width):
        return pl.ds(pl.multiple_of(index * width, width), width)

    mask_float = mask[...].astype(F32)
    first = mask_float * obs[...]
    held[0, tm, pl.ds(0, rows), :] = first
    held[0, tm, pl.ds(rows, SCALARS), :] = jnp.zeros((SCALARS, cols), F32)

    own_stamps = stamps[:, lanes(tm, cols)]

    def time_part(k, carry):
        there = lanes(k, cols)
        distance = jnp.abs(column_of(stamps[:, there], cols) - own_stamps)
        high, low = split(matern_of(distance, time_length))
        kt[0, there, :] = high
        kt[1, there, :] = low
        return carry

    lax.fori_loop(0, n_tm, time_part, 0)

    pl.semaphore_wait(barrier, n_tm - 1 + n_loc - 1)

    def send_held(turn):
        for d, peer in enumerate(tm_peers):
            send(held.at[turn], tm, held_send.at[turn, d], held_recv.at[turn], {"tm": peer})

    def fold(turn):
        def part(slot):
            high, low = split(held[turn, slot, pl.ds(0, rows), :])
            there = lanes(slot, cols)
            return dot3(high, low, kt[0, there, :], kt[1, there, :])

        total = part(tm)
        scalars = held[turn, tm, pl.ds(rows, SCALARS), :]
        for d, peer in enumerate(tm_peers):
            arrived(held.at[turn], peer, held_recv.at[turn], held_send.at[turn, d])
            total += part(peer)
            scalars += held[turn, peer, pl.ds(rows, SCALARS), :]
        inner[turn, loc, pl.ds(0, rows), :] = total
        inner[turn, loc, pl.ds(rows, SCALARS), :] = scalars

    def send_inner(turn):
        send(inner.at[turn], loc, inner_send.at[turn, 0], inner_recv.at[turn], {"loc": sibling})
        for d, peer in enumerate(mates):
            send(inner.at[turn], loc, inner_send.at[turn, d + 1], inner_recv.at[turn], {"loc": peer})

    def mix(turn):
        def part(slot):
            high, low = split(inner[turn, slot, pl.ds(0, rows), :])
            there = lanes(slot, rows)
            return dot3(ks[0, :, there], ks[1, :, there], high, low)

        def scalars_of(slot):
            return inner[turn, slot, pl.ds(rows, SCALARS), :]

        total, scalars = part(loc), scalars_of(loc)
        arrived(inner.at[turn], sibling, inner_recv.at[turn], inner_send.at[turn, 0])
        total, scalars = total + part(sibling), scalars + scalars_of(sibling)
        for d, peer in enumerate(mates):
            arrived(inner.at[turn], peer, inner_recv.at[turn], inner_send.at[turn, 0])
            send(inner.at[turn], peer, pass_send.at[turn, d], inner_recv.at[turn], {"loc": sibling})
            total, scalars = total + part(peer), scalars + scalars_of(peer)
        for d, peer in enumerate(mates):
            slot = (peer - core) + (1 - core)
            arrived(inner.at[turn], slot, inner_recv.at[turn], inner_send.at[turn, 0])
            total, scalars = total + part(slot), scalars + scalars_of(slot)
        return total, scalars

    def predict(turn):
        def part(slot, total):
            high, low = split(inner[turn, slot, pl.ds(0, rows), :])
            there = lanes(slot, rows)
            return total + dot3(kx[0, :, there], kx[1, :, there], high, low)

        return lax.fori_loop(0, n_loc, part, jnp.zeros((rows, cols), F32))

    def space_kernel(out, x_column, y_column):
        def part(k, carry):
            there = lanes(k, rows)
            dx = x_column - pos[0:1, there]
            dy = y_column - pos[1:2, there]
            high, low = split(matern_of(jnp.sqrt(dx * dx + dy * dy), space_length))
            out[0, :, there] = high
            out[1, :, there] = low
            return carry

        lax.fori_loop(0, n_loc, part, 0)

    send_held(0)
    own = lanes(loc, rows)
    space_kernel(ks, column_of(pos[0:1, own], rows), column_of(pos[1:2, own], rows))
    fold(0)
    send_inner(0)

    wanted = column_of(order[:, own].astype(F32), rows)
    lane = lax.broadcasted_iota(jnp.int32, (rows, rows), 1).astype(F32)

    def pick(k, carry):
        x, y = carry
        there = lanes(k, rows)
        hit = wanted == lane + lax.convert_element_type(k * rows, F32)
        x += jnp.where(hit, test[0:1, there], 0.0)
        y += jnp.where(hit, test[1:2, there], 0.0)
        return x, y

    zero = jnp.zeros((rows, rows), F32)
    x_test, y_test = lax.fori_loop(0, test.shape[1] // rows, pick, (zero, zero))
    x_test = jnp.sum(x_test, axis=1, keepdims=True)
    y_test = jnp.sum(y_test, axis=1, keepdims=True)
    space_kernel(kx, x_test, y_test)

    noise_row = noise[...]
    outer, _ = mix(0)
    image = mask_float * outer * amplitude + first * noise_row

    held[1, tm, pl.ds(0, rows), :] = image
    held[1, tm, pl.ds(rows, SCALARS), :] = lane_sums(first * first, first * image, image * image)
    send_held(1)
    predicted_first = predict(0)
    fold(1)
    send_inner(1)
    outer, scalars = mix(1)
    image_image = mask_float * outer * amplitude + image * noise_row

    sums = jnp.sum(scalars, axis=1, keepdims=True)
    norm, curvature, image_norm = sums[0:1], sums[1:2], sums[2:3]
    step = norm / curvature
    ratio = jnp.maximum(step * (step * image_norm) - norm, 0.0) / norm
    residual = first - step * image
    direction = residual + ratio * first
    direction_image = (image - step * image_image) + ratio * image

    red_t[tm] = lane_sums(residual * residual, direction * direction_image)
    for d, peer in enumerate(tm_peers):
        send(red_t, tm, rt_send.at[d], rt_recv, {"tm": peer})
    predicted_image = predict(1)
    for d, peer in enumerate(tm_peers):
        arrived(red_t, peer, rt_recv, rt_send.at[d])
    red_l[loc] = jnp.sum(red_t[...], axis=0)
    for d, peer in enumerate(loc_peers):
        send(red_l, loc, rl_send.at[d], rl_recv, {"loc": peer})
    for d, peer in enumerate(loc_peers):
        arrived(red_l, peer, rl_recv, rl_send.at[d])
    sums = jnp.sum(jnp.sum(red_l[...], axis=0), axis=1, keepdims=True)
    last_step = sums[0:1] / sums[1:2]

    est[...] = step * first + last_step * direction
    on_first = amplitude * (step + last_step * (1.0 + ratio))
    on_image = amplitude * (-last_step * step)
    post[...] = on_first * predicted_first + on_image * predicted_image
    for copy in started:
        copy.wait_send()


def solution(mesh):
    n_loc, n_tm = mesh.shape["loc"], mesh.shape["tm"]

    def on_device(observed, observed_mask, positions, time_stamps, noise_var, test_coords, site_order):
        rows, cols = observed.shape
        locs, times = positions.shape[1], time_stamps.shape[0]
        block = jax.ShapeDtypeStruct((rows, cols), F32)
        vmem = pl.BlockSpec(memory_space=pltpu.VMEM)
        dma = pltpu.SemaphoreType.DMA
        return pl.pallas_call(
            functools.partial(kernel, n_loc, n_tm),
            out_shape=(block, block),
            in_specs=[vmem] * 7,
            out_specs=(vmem, vmem),
            scratch_shapes=[
                pltpu.VMEM((2, n_tm, rows + SCALARS, cols), F32),
                pltpu.VMEM((2, n_loc, rows + SCALARS, cols), F32),
                pltpu.VMEM((n_tm, SCALARS, cols), F32),
                pltpu.VMEM((n_loc, SCALARS, cols), F32),
                pltpu.VMEM((2, rows, locs), BF16),
                pltpu.VMEM((2, rows, locs), BF16),
                pltpu.VMEM((2, times, cols), BF16),
                dma((2, n_tm)), dma((2, n_tm)),
                dma((2, n_loc)), dma((2, n_loc)), dma((2, n_loc)),
                dma((n_tm,)), dma((n_tm,)),
                dma((n_loc,)), dma((n_loc,)),
            ],
            compiler_params=pltpu.CompilerParams(
                collective_id=0, has_side_effects=True, vmem_limit_bytes=32 * 1024 * 1024
            ),
        )(
            observed, observed_mask, positions, time_stamps[None, :], noise_var[None, :],
            test_coords, site_order[None, :],
        )

    in_specs = (P("loc", "tm"), P("loc", "tm"), P(), P(), P("tm"), P(), P())
    out_specs = (P("loc", "tm"), P("loc", "tm"))
    return jax.shard_map(on_device, mesh=mesh, in_specs=in_specs, out_specs=out_specs, check_vma=False)
```

time: 253 us -> 47.7 us (0.19)
  blocking collectives: 185 us -> 0 us
  Pallas kernels: 0 us -> 41 us
  waiting for transfers between devices: 33.9 us -> 0 us
  between operations: 18.1 us -> 0.66 us
  matrix products: 6.23 us -> 0 us
  other arithmetic: 3.53 us -> 0 us
    psum x3 -> x0, blocking collectives: 119 us -> none  [the longest x2 81.4 us: squares(): return lax.psum(jnp.sum(residual * residual), ('loc', 'tm'))]
    all_gather x5 -> x0, blocking collectives: 65.2 us -> none  [the longest x2 29.8 us: on_device(): inner = time_fold(lax.all_gather(masked, 'tm', axis=1, tiled=True))]
    pallas_call x0 -> x1, Pallas kernels: none -> 41 us  [on_device(): pl.pallas_call(functools.partial(kernel, n_loc, n_tm), out_shape=(block,...]
    reduce_scatter x1 -> x0, waiting for transfers between devices: 33.9 us -> none  [on_device(): lax.psum_scatter(between_covariance_block(unseen_site_positions, own_poin...]
    dot_general x6 -> x0, matrix products: 6.23 us -> none  [the longest x2 2.94 us: add_block(): jnp.dot(kernel, rows_part, precision=lax.Precision.HIGHEST, preferred_ele...]
    gather x2 -> x0, local copies, waits for them, and re-layouts: 2.99 us -> none  [on_device(): unseen_site_positions = test_coords[:, site_order]]
    unnamed x15 -> x16, local copies, waits for them, and re-layouts: 2.84 us -> 5.69 us
  transfers between devices with their start and end apart: 1 -> 0, of which waited for: 1 -> 0; matrix products, arithmetic and copies ran while one was open for 0% -> 0% of each run, Pallas kernels for 0% -> 0%
where the time goes in v1:
time: 47.7 us; the launch traced here: 47.4 us
  Pallas kernels  41 us (86%)
  local copies, waits for them, and re-layouts  5.69 us (12%)
  between operations  0.66 us (1%)
    pallas_call x1, Pallas kernels, on_device(): pl.pallas_call(functools.partial(kernel, n_loc, n_tm), out_shape=(block,...  41 us
    unnamed x16, local copies, waits for them, and re-layouts  5.69 us

profile of v1, /device:TPU:0, one launch (start us, length us, event | category | flops | bytes accessed | tf_op | source)
XLA Modules:
  0.0 47.4 jit_solution(14497849364238840931)
XLA Ops:
  0.6 0.0 copy-start.4
  0.6 0.0 copy-start.6
  0.7 0.7 %copy-done.4 = s32[1024]{0:T(1024)S(1)} copy-done((s32[1024]{0:T(1024)S(1)}, s32[1024]{0:T(1024)}, u32[]{:S(2)}) %copy-start.4) | copy-done | bytes 4120
  1.3 0.0 copy-done.6
  1.3 0.0 copy-start
  1.3 0.8 %copy-done = f32[128,128]{1,0:T(8,128)S(1)} copy-done((f32[128,128]{1,0:T(8,128)S(1)}, f32[128,128]{1,0:T(8,128)}, u32[]{:S(2)}) %copy-start) | copy-done | bytes 65560
  2.2 0.0 copy-start.1
  2.2 0.8 %copy-done.1 = s32[128,128]{1,0:T(8,128)S(1)} copy-done((s32[128,128]{1,0:T(8,128)S(1)}, s32[128,128]{1,0:T(8,128)}, u32[]{:S(2)}) %copy-start.1) | copy-done | bytes 65560
  3.0 0.0 copy-start.2
  3.0 0.7 %copy-done.2 = f32[2,1024]{1,0:T(2,128)S(1)} copy-done((f32[2,1024]{1,0:T(2,128)S(1)}, f32[2,1024]{1,0:T(2,128)}, u32[]{:S(2)}) %copy-start.2) | copy-done | bytes 8216
  3.7 0.0 copy-start.3
  3.7 0.7 %copy-done.3 = f32[2,1024]{1,0:T(2,128)S(1)} copy-done((f32[2,1024]{1,0:T(2,128)S(1)}, f32[2,1024]{1,0:T(2,128)}, u32[]{:S(2)}) %copy-start.3) | copy-done | bytes 8216
  4.4 0.0 copy-start.5
  4.4 0.7 %copy-done.5 = f32[512]{0:T(512)S(1)} copy-done((f32[512]{0:T(512)S(1)}, f32[512]{0:T(512)}, u32[]{:S(2)}) %copy-start.5) | copy-done | bytes 2072
  5.1 41.0 %shard_map.86 = (f32[128,128]{1,0:T(8,128)S(1)}, f32[128,128]{1,0:T(8,128)S(1)}) custom-call(f32[128,128]{1,0:T(8,128)S(1)} %copy-done, s32[128,128]{1,0:T(8,128)S(1)} %copy-done.1, f32[2,1024]{1,0:T(2,128)S(1)} %copy-done.2, f32[1,512]{1,0:T(1,128)S(1)} %bitcast.4, f32[1,128]{1,0:T(1,128)S(1)} %bitcast.5, f32[2,1024]{1,0:T(2,128)S(1)} %copy-done.3, ...), custom_call_target="tpu_custom_call" | custom-call | tf_op jit(solution)/shard_map/pallas_call | solution.py:261
  46.1 0.6 %copy.11 = f32[128,128]{1,0:T(8,128)} copy(f32[128,128]{1,0:T(8,128)S(1)} %get-tuple-element.4) | data formatting | bytes 131072
  46.7 0.6 %copy.12 = f32[128,128]{1,0:T(8,128)} copy(f32[128,128]{1,0:T(8,128)S(1)} %get-tuple-element.5) | data formatting | bytes 131072
Async XLA Ops:
  0.6 0.7 %copy-start.4 = (s32[1024]{0:T(1024)S(1)}, s32[1024]{0:T(1024)}, u32[]{:S(2)}) copy-start(s32[1024]{0:T(1024)} %param.13) | copy-start | bytes 12292
  0.6 0.7 %copy-start.6 = (f32[128]{0:T(128)S(1)}, f32[128]{0:T(128)}, u32[]{:S(2)}) copy-start(f32[128]{0:T(128)} %param.11) | copy-start | bytes 1540
  1.3 0.8 %copy-start = (f32[128,128]{1,0:T(8,128)S(1)}, f32[128,128]{1,0:T(8,128)}, u32[]{:S(2)}) copy-start(f32[128,128]{1,0:T(8,128)} %obs.1) | copy-start | bytes 196612
  2.2 0.8 %copy-start.1 = (s32[128,128]{1,0:T(8,128)S(1)}, s32[128,128]{1,0:T(8,128)}, u32[]{:S(2)}) copy-start(s32[128,128]{1,0:T(8,128)} %mask.1) | copy-start | bytes 196612
  3.0 0.7 %copy-start.2 = (f32[2,1024]{1,0:T(2,128)S(1)}, f32[2,1024]{1,0:T(2,128)}, u32[]{:S(2)}) copy-start(f32[2,1024]{1,0:T(2,128)} %pos.1) | copy-start | bytes 24580
  3.7 0.7 %copy-start.3 = (f32[2,1024]{1,0:T(2,128)S(1)}, f32[2,1024]{1,0:T(2,128)}, u32[]{:S(2)}) copy-start(f32[2,1024]{1,0:T(2,128)} %test.1) | copy-start | bytes 24580
  4.4 0.7 %copy-start.5 = (f32[512]{0:T(512)S(1)}, f32[512]{0:T(512)}, u32[]{:S(2)}) copy-start(f32[512]{0:T(512)} %param.10) | copy-start | bytes 6148

commit v2 on v1

v2 whole, which is shorter than its diff:
```python
import functools
import math

import jax
import jax.numpy as jnp
from jax import lax
from jax.experimental import pallas as pl
from jax.experimental.pallas import tpu as pltpu
from jax.sharding import PartitionSpec as P

MESH = pl.DeviceIdType.MESH
F32 = jnp.float32
BF16 = jnp.bfloat16

root_three = math.sqrt(3.0)
space_reach = 2.5
time_reach = 5.0
amplitude = 0.1
SCALARS = 8
CHUNKS = 2


def split(x):
    high = x.astype(BF16)
    return high, (x - high.astype(F32)).astype(BF16)


def dot(a, b):
    return jnp.dot(a, b, preferred_element_type=F32)


def dot3(a_high, a_low, b_high, b_low):
    return dot(a_high, b_high) + (dot(a_high, b_low) + dot(a_low, b_high))


def column_of(row, width):
    return jnp.transpose(jnp.broadcast_to(row, (width, row.shape[1])))


def matern_of(distance, length):
    scaled = distance * (root_three / length)
    return (1.0 + scaled) * jnp.exp(-scaled)


def lane_sums(*arrays):
    sums = [jnp.sum(a, axis=0, keepdims=True) for a in arrays]
    sums.append(jnp.zeros((SCALARS - len(sums), sums[0].shape[1]), F32))
    return jnp.concatenate(sums, axis=0)


def other(index, step, count):
    if count & (count - 1):
        return lax.rem(index + step, count)
    bit = 1
    while bit < count:
        if step & bit:
            index = index + bit * (1 - 2 * lax.rem(index // bit, 2))
        bit *= 2
    return index


def kernel(
    n_loc, n_tm,
    obs_hbm, mask_hbm, pos_hbm, stamps_hbm, noise_hbm, test_hbm, order_hbm,
    est, post,
    obs, mask, pos, stamps, noise, test, order, arg_sem,
    held, inner, red, kk, kt,
    held_send, held_recv, inner_send, inner_recv, pass_send, red_send, red_recv,
):
    loc, tm = lax.axis_index("loc"), lax.axis_index("tm")
    rows, cols = obs.shape
    n_chip = n_loc // 2
    chip, core = loc // 2, lax.rem(loc, 2)
    sibling = chip * 2 + (1 - core)
    space_length = space_reach / math.sqrt(pos.shape[1])
    time_length = time_reach / stamps.shape[1]
    tm_peers = [other(tm, d, n_tm) for d in range(n_tm - 1, 0, -1)]
    loc_peers = [other(loc, d, n_loc) for d in range(n_loc - 1, 0, -1)]
    mates = [other(chip, d, n_chip) * 2 + core for d in range(n_chip - 1, 0, -1)]
    chunk = rows // CHUNKS
    chunks = [
        pl.ds(h * chunk, chunk + (SCALARS if h == CHUNKS - 1 else 0)) for h in range(CHUNKS)
    ]
    started = []

    arguments = (
        (stamps_hbm, stamps), (obs_hbm, obs), (mask_hbm, mask), (pos_hbm, pos),
        (test_hbm, test), (order_hbm, order), (noise_hbm, noise),
    )
    loads = [
        pltpu.make_async_copy(there, here, arg_sem.at[k]) for k, (there, here) in enumerate(arguments)
    ]
    for load in loads:
        load.start()

    barrier = pltpu.get_barrier_semaphore()
    for peer in tm_peers:
        pl.semaphore_signal(barrier, inc=1, device_id={"tm": peer}, device_id_type=MESH)
    for peer in loc_peers:
        pl.semaphore_signal(barrier, inc=1, device_id={"loc": peer}, device_id_type=MESH)

    def copy_of(ref, slot, h, send_sem, recv_sem, where):
        block = ref.at[slot, chunks[h], :]
        return pltpu.make_async_remote_copy(
            src_ref=block,
            dst_ref=block,
            send_sem=send_sem,
            recv_sem=recv_sem.at[slot, h],
            device_id=where,
            device_id_type=MESH,
        )

    def send(*how):
        copy = copy_of(*how)
        copy.start()
        started.append(copy)

    def lanes(index, width):
        return pl.ds(pl.multiple_of(index * width, width), width)

    loads[0].wait()
    loads[1].wait()
    loads[2].wait()
    mask_float = mask[...].astype(F32)
    first = mask_float * obs[...]
    held[0, tm, pl.ds(0, rows), :] = first
    held[0, tm, pl.ds(rows, SCALARS), :] = jnp.zeros((SCALARS, cols), F32)

    own_stamps = stamps[:, lanes(tm, cols)]

    def time_part(k, carry):
        there = lanes(k, cols)
        distance = jnp.abs(column_of(stamps[:, there], cols) - own_stamps)
        high, low = split(matern_of(distance, time_length))
        kt[0, there, :] = high
        kt[1, there, :] = low
        return carry

    lax.fori_loop(0, n_tm, time_part, 0)

    pl.semaphore_wait(barrier, n_tm - 1 + n_loc - 1)

    def send_held(turn):
        for h in range(CHUNKS):
            for d, peer in enumerate(tm_peers):
                send(held.at[turn], tm, h, held_send.at[turn, d, h], held_recv.at[turn], {"tm": peer})

    def fold(turn):
        scalars = held[turn, tm, pl.ds(rows, SCALARS), :]
        for h in range(CHUNKS):
            these = pl.ds(h * chunk, chunk)

            def part(slot):
                high, low = split(held[turn, slot, these, :])
                there = lanes(slot, cols)
                return dot3(high, low, kt[0, there, :], kt[1, there, :])

            total = part(tm)
            for d, peer in reversed(list(enumerate(tm_peers))):
                copy_of(
                    held.at[turn], peer, h, held_send.at[turn, d, h], held_recv.at[turn], {"tm": peer}
                ).wait_recv()
                total += part(peer)
                if h == CHUNKS - 1:
                    scalars += held[turn, peer, pl.ds(rows, SCALARS), :]
            inner[turn, loc, these, :] = total
            if h == CHUNKS - 1:
                inner[turn, loc, pl.ds(rows, SCALARS), :] = scalars
            for d, peer in enumerate(mates + [sibling]):
                send(inner.at[turn], loc, h, inner_send.at[turn, d, h], inner_recv.at[turn], {"loc": peer})

    def mix(turn):
        def part(slot):
            high, low = split(inner[turn, slot, pl.ds(0, rows), :])
            there = lanes(slot, rows)
            return dot3(kk[0, :, there], kk[1, :, there], high, low)

        def scalars_of(slot):
            return inner[turn, slot, pl.ds(rows, SCALARS), :]

        def arrived(slot, h):
            copy_of(
                inner.at[turn], slot, h, inner_send.at[turn, 0, 0], inner_recv.at[turn], {"loc": sibling}
            ).wait_recv()

        total, scalars = part(loc), scalars_of(loc)
        for h in range(CHUNKS):
            arrived(sibling, h)
        total, scalars = total + part(sibling), scalars + scalars_of(sibling)
        for h in range(CHUNKS):
            for d, peer in enumerate(mates):
                arrived(peer, h)
                send(inner.at[turn], peer, h, pass_send.at[turn, d, h], inner_recv.at[turn], {"loc": sibling})
        for peer in mates:
            total, scalars = total + part(peer), scalars + scalars_of(peer)
        for peer in mates:
            slot = (peer - core) + (1 - core)
            for h in range(CHUNKS):
                arrived(slot, h)
            total, scalars = total + part(slot), scalars + scalars_of(slot)
        return total[:rows], total[rows:], scalars

    def space_kernel(these, x_column, y_column):
        def part(k, carry):
            there = lanes(k, rows)
            dx = x_column - pos[0:1, there]
            dy = y_column - pos[1:2, there]
            high, low = split(matern_of(jnp.sqrt(dx * dx + dy * dy), space_length))
            kk[0, these, there] = high
            kk[1, these, there] = low
            return carry

        lax.fori_loop(0, n_loc, part, 0)

    send_held(0)
    for load in loads[3:]:
        load.wait()
    own = lanes(loc, rows)
    space_kernel(pl.ds(0, rows), column_of(pos[0:1, own], rows), column_of(pos[1:2, own], rows))
    fold(0)

    wanted = column_of(order[:, own].astype(F32), rows)
    lane = lax.broadcasted_iota(jnp.int32, (rows, rows), 1).astype(F32)

    def pick(k, carry):
        x, y = carry
        there = lanes(k, rows)
        hit = wanted == lane + lax.convert_element_type(k * rows, F32)
        x += jnp.where(hit, test[0:1, there], 0.0)
        y += jnp.where(hit, test[1:2, there], 0.0)
        return x, y

    zero = jnp.zeros((rows, rows), F32)
    x_test, y_test = lax.fori_loop(0, test.shape[1] // rows, pick, (zero, zero))
    x_test = jnp.sum(x_test, axis=1, keepdims=True)
    y_test = jnp.sum(y_test, axis=1, keepdims=True)
    space_kernel(pl.ds(rows, rows), x_test, y_test)

    noise_row = noise[...]
    outer, predicted_first, _ = mix(0)
    image = mask_float * outer * amplitude + first * noise_row

    held[1, tm, pl.ds(0, rows), :] = image
    held[1, tm, pl.ds(rows, SCALARS), :] = lane_sums(first * first, first * image, image * image)
    send_held(1)
    fold(1)
    outer, predicted_image, scalars = mix(1)
    image_image = mask_float * outer * amplitude + image * noise_row

    sums = jnp.sum(scalars, axis=1, keepdims=True)
    norm, curvature, image_norm = sums[0:1], sums[1:2], sums[2:3]
    step = norm / curvature
    ratio = jnp.maximum(step * (step * image_norm) - norm, 0.0) / norm
    residual = first - step * image
    direction = residual + ratio * first
    direction_image = (image - step * image_image) + ratio * image

    red[0] = lane_sums(residual * residual, direction * direction_image)
    far = [(a, b) for b in range(n_tm - 1, -1, -1) for a in range(n_loc - 1, -1, -1) if a or b]
    for k, (a, b) in enumerate(far):
        copy = pltpu.make_async_remote_copy(
            src_ref=red.at[0],
            dst_ref=red.at[k + 1],
            send_sem=red_send.at[k],
            recv_sem=red_recv,
            device_id=(other(loc, a, n_loc) if a else loc, other(tm, b, n_tm) if b else tm),
            device_id_type=MESH,
        )
        copy.start()
        started.append(copy)
    others = red.at[pl.ds(1, len(far))]
    pltpu.make_async_remote_copy(
        src_ref=others,
        dst_ref=others,
        send_sem=red_send.at[0],
        recv_sem=red_recv,
        device_id={"loc": sibling},
        device_id_type=MESH,
    ).wait_recv()
    sums = jnp.sum(jnp.sum(red[...], axis=0), axis=1, keepdims=True)
    last_step = sums[0:1] / sums[1:2]

    est[...] = step * first + last_step * direction
    on_first = amplitude * (step + last_step * (1.0 + ratio))
    on_image = amplitude * (-last_step * step)
    post[...] = on_first * predicted_first + on_image * predicted_image
    for copy in started:
        copy.wait_send()


def solution(mesh):
    n_loc, n_tm = mesh.shape["loc"], mesh.shape["tm"]

    def on_device(observed, observed_mask, positions, time_stamps, noise_var, test_coords, site_order):
        rows, cols = observed.shape
        locs, times = positions.shape[1], time_stamps.shape[0]
        block = jax.ShapeDtypeStruct((rows, cols), F32)
        vmem = pl.BlockSpec(memory_space=pltpu.VMEM)
        dma = pltpu.SemaphoreType.DMA
        return pl.pallas_call(
            functools.partial(kernel, n_loc, n_tm),
            out_shape=(block, block),
            in_specs=[pl.BlockSpec(memory_space=pltpu.HBM)] * 7,
            out_specs=(vmem, vmem),
            scratch_shapes=[
                pltpu.VMEM((rows, cols), F32),
                pltpu.VMEM((rows, cols), jnp.int32),
                pltpu.VMEM((2, locs), F32),
                pltpu.VMEM((1, times), F32),
                pltpu.VMEM((1, cols), F32),
                pltpu.VMEM(test_coords.shape, F32),
                pltpu.VMEM((1, site_order.shape[0]), jnp.int32),
                dma((7,)),
                pltpu.VMEM((2, n_tm, rows + SCALARS, cols), F32),
                pltpu.VMEM((2, n_loc, rows + SCALARS, cols), F32),
                pltpu.VMEM((n_loc * n_tm, SCALARS, cols), F32),
                pltpu.VMEM((2, 2 * rows, locs), BF16),
                pltpu.VMEM((2, times, cols), BF16),
                dma((2, n_tm, CHUNKS)), dma((2, n_tm, CHUNKS)),
                dma((2, n_loc, CHUNKS)), dma((2, n_loc, CHUNKS)), dma((2, n_loc, CHUNKS)),
                dma((n_loc * n_tm,)), dma(()),
            ],
            compiler_params=pltpu.CompilerParams(
                collective_id=0, has_side_effects=True, vmem_limit_bytes=60 * 1024 * 1024
            ),
        )(
            observed, observed_mask, positions, time_stamps[None, :], noise_var[None, :],
            test_coords, site_order[None, :],
        )

    in_specs = (P("loc", "tm"), P("loc", "tm"), P(), P(), P("tm"), P(), P())
    out_specs = (P("loc", "tm"), P("loc", "tm"))
    return jax.shard_map(on_device, mesh=mesh, in_specs=in_specs, out_specs=out_specs, check_vma=False)
```

time: 47.7 us -> 40.6 us (0.85)
  local copies, waits for them, and re-layouts: 5.69 us -> 2.14 us
  Pallas kernels: 41 us -> 37.6 us
    unnamed x16 -> x4, local copies, waits for them, and re-layouts: 5.69 us -> 2.14 us
    pallas_call x1, Pallas kernels: 41 us -> 37.6 us  [on_device(): pl.pallas_call(functools.partial(kernel, n_loc, n_tm), out_shape=(block,...]
where the time goes in v2:
time: 40.6 us; the launch traced here: 40.4 us
  Pallas kernels  37.6 us (93%)
  local copies, waits for them, and re-layouts  2.14 us (5%)
  between operations  0.65 us (2%)
    pallas_call x1, Pallas kernels, on_device(): pl.pallas_call(functools.partial(kernel, n_loc, n_tm), out_shape=(block,...  37.6 us
    unnamed x4, local copies, waits for them, and re-layouts  2.14 us

profile of v2, /device:TPU:0, one launch (start us, length us, event | category | flops | bytes accessed | tf_op | source)
XLA Modules:
  0.0 40.4 jit_solution(3580164885798383270)
XLA Ops:
  0.6 37.6 %shard_map.86 = (f32[128,128]{1,0:T(8,128)}, f32[128,128]{1,0:T(8,128)}) custom-call(f32[128,128]{1,0:T(8,128)} %obs_hbm.1, s32[128,128]{1,0:T(8,128)} %mask_hbm.1, f32[2,1024]{1,0:T(2,128)} %pos_hbm.1, f32[1,512]{1,0:T(1,128)} %bitcast.4, f32[1,128]{1,0:T(1,128)} %bitcast.5, f32[2,1024]{1,0:T(2,128)} %test_hbm.1, s32[1,1024]{1,0:T(1,128)} %bitcast.3), custom_call_target="tpu_custom_call" | custom-call | tf_op jit(solution)/shard_map/pallas_call | solution.py:300
  38.2 0.0 copy-start
  38.2 1.5 %copy.11 = f32[128,128]{1,0:T(8,128)} copy(f32[128,128]{1,0:T(8,128)} %get-tuple-element.4) | data formatting | bytes 131072
  39.7 0.0 copy-done
  39.7 0.6 %copy.12 = f32[128,128]{1,0:T(8,128)} copy(f32[128,128]{1,0:T(8,128)S(1)} %copy-done) | data formatting | bytes 131072
Async XLA Ops:
  38.2 1.5 %copy-start = (f32[128,128]{1,0:T(8,128)S(1)}, f32[128,128]{1,0:T(8,128)}, u32[]{:S(2)}) copy-start(f32[128,128]{1,0:T(8,128)} %get-tuple-element.5) | copy-start | bytes 196612

commit v3 on v2

--- a/solution.py
+++ b/solution.py
@@ -17,7 +17,8 @@
 time_reach = 5.0
 amplitude = 0.1
 SCALARS = 8
-CHUNKS = 2
+SIXTEENTHS = (0, 8, 16)
+CHUNKS = len(SIXTEENTHS) - 1
 
 
 def split(x):
@@ -50,7 +51,8 @@
 
 def other(index, step, count):
     if count & (count - 1):
-        return lax.rem(index + step, count)
+        return lax.rem(index + step + count, count)
+    step = abs(step)
     bit = 1
     while bit < count:
         if step & bit:
@@ -76,12 +78,18 @@
     time_length = time_reach / stamps.shape[1]
     tm_peers = [other(tm, d, n_tm) for d in range(n_tm - 1, 0, -1)]
     loc_peers = [other(loc, d, n_loc) for d in range(n_loc - 1, 0, -1)]
-    mates = [other(chip, d, n_chip) * 2 + core for d in range(n_chip - 1, 0, -1)]
-    chunk = rows // CHUNKS
-    chunks = [
-        pl.ds(h * chunk, chunk + (SCALARS if h == CHUNKS - 1 else 0)) for h in range(CHUNKS)
-    ]
+    near = []
+    far = list(range(n_chip - 1, 0, -1))
+    starts = [rows * part // 16 for part in SIXTEENTHS]
+    parts = [pl.ds(starts[h], starts[h + 1] - starts[h]) for h in range(CHUNKS)]
+    chunks = parts[:-1] + [pl.ds(starts[-2], rows + SCALARS - starts[-2])]
     started = []
+
+    barrier = pltpu.get_barrier_semaphore()
+    for peer in tm_peers:
+        pl.semaphore_signal(barrier, inc=1, device_id={"tm": peer}, device_id_type=MESH)
+    for peer in loc_peers:
+        pl.semaphore_signal(barrier, inc=1, device_id={"loc": peer}, device_id_type=MESH)
 
     arguments = (
         (stamps_hbm, stamps), (obs_hbm, obs), (mask_hbm, mask), (pos_hbm, pos),
@@ -92,12 +100,6 @@
     ]
     for load in loads:
         load.start()
-
-    barrier = pltpu.get_barrier_semaphore()
-    for peer in tm_peers:
-        pl.semaphore_signal(barrier, inc=1, device_id={"tm": peer}, device_id_type=MESH)
-    for peer in loc_peers:
-        pl.semaphore_signal(barrier, inc=1, device_id={"loc": peer}, device_id_type=MESH)
 
     def copy_of(ref, slot, h, send_sem, recv_sem, where):
         block = ref.at[slot, chunks[h], :]
@@ -148,7 +150,7 @@
     def fold(turn):
         scalars = held[turn, tm, pl.ds(rows, SCALARS), :]
         for h in range(CHUNKS):
-            these = pl.ds(h * chunk, chunk)
+            these = parts[h]
 
             def part(slot):
                 high, low = split(held[turn, slot, these, :])
@@ -166,7 +168,11 @@
             inner[turn, loc, these, :] = total
             if h == CHUNKS - 1:
                 inner[turn, loc, pl.ds(rows, SCALARS), :] = scalars
-            for d, peer in enumerate(mates + [sibling]):
+            targets = [other(chip, d, n_chip) * 2 + core for d in far]
+            for d in near:
+                there = other(chip, d, n_chip) * 2
+                targets += [there + core, there + (1 - core)]
+            for d, peer in enumerate(targets + [sibling]):
                 send(inner.at[turn], loc, h, inner_send.at[turn, d, h], inner_recv.at[turn], {"loc": peer})
 
     def mix(turn):
@@ -183,18 +189,22 @@
                 inner.at[turn], slot, h, inner_send.at[turn, 0, 0], inner_recv.at[turn], {"loc": sibling}
             ).wait_recv()
 
+        passed = [other(chip, -d, n_chip) * 2 for d in far]
+        direct = [other(chip, -d, n_chip) * 2 for d in near]
+        for h in range(CHUNKS):
+            for d, pair in enumerate(passed):
+                arrived(pair + core, h)
+                send(
+                    inner.at[turn], pair + core, h, pass_send.at[turn, d, h], inner_recv.at[turn],
+                    {"loc": sibling},
+                )
         total, scalars = part(loc), scalars_of(loc)
         for h in range(CHUNKS):
             arrived(sibling, h)
-        total, scalars = total + part(sibling), scalars + scalars_of(sibling)
-        for h in range(CHUNKS):
-            for d, peer in enumerate(mates):
-                arrived(peer, h)
-                send(inner.at[turn], peer, h, pass_send.at[turn, d, h], inner_recv.at[turn], {"loc": sibling})
-        for peer in mates:
-            total, scalars = total + part(peer), scalars + scalars_of(peer)
-        for peer in mates:
-            slot = (peer - core) + (1 - core)
+        for slot in [sibling] + [pair + core for pair in passed]:
+            total, scalars = total + part(slot), scalars + scalars_of(slot)
+        last = [pair + k for pair in direct for k in (0, 1)] + [pair + (1 - core) for pair in passed]
+        for slot in last:
             for h in range(CHUNKS):
                 arrived(slot, h)
             total, scalars = total + part(slot), scalars + scalars_of(slot)
@@ -256,8 +266,8 @@
     direction_image = (image - step * image_image) + ratio * image
 
     red[0] = lane_sums(residual * residual, direction * direction_image)
-    far = [(a, b) for b in range(n_tm - 1, -1, -1) for a in range(n_loc - 1, -1, -1) if a or b]
-    for k, (a, b) in enumerate(far):
+    away = [(a, b) for b in range(n_tm - 1, -1, -1) for a in range(n_loc - 1, -1, -1) if a or b]
+    for k, (a, b) in enumerate(away):
         copy = pltpu.make_async_remote_copy(
             src_ref=red.at[0],
             dst_ref=red.at[k + 1],
@@ -268,7 +278,7 @@
         )
         copy.start()
         started.append(copy)
-    others = red.at[pl.ds(1, len(far))]
+    others = red.at[pl.ds(1, len(away))]
     pltpu.make_async_remote_copy(
         src_ref=others,
         dst_ref=others,
@@ -294,12 +304,11 @@
     def on_device(observed, observed_mask, positions, time_stamps, noise_var, test_coords, site_order):
         rows, cols = observed.shape
         locs, times = positions.shape[1], time_stamps.shape[0]
-        block = jax.ShapeDtypeStruct((rows, cols), F32)
         vmem = pl.BlockSpec(memory_space=pltpu.VMEM)
         dma = pltpu.SemaphoreType.DMA
         return pl.pallas_call(
             functools.partial(kernel, n_loc, n_tm),
-            out_shape=(block, block),
+            out_shape=(pltpu.VMEM((rows, cols), F32), pltpu.VMEM((rows, cols), F32)),
             in_specs=[pl.BlockSpec(memory_space=pltpu.HBM)] * 7,
             out_specs=(vmem, vmem),
             scratch_shapes=[

time: 40.6 us -> 39.2 us (0.966)
  local copies, waits for them, and re-layouts: 2.14 us -> 1.26 us
  Pallas kernels: 37.6 us -> 37.1 us
    unnamed x4 -> x2, local copies, waits for them, and re-layouts: 2.14 us -> 1.26 us
    pallas_call x1, Pallas kernels: 37.6 us -> 37.1 us  [on_device(): pl.pallas_call(functools.partial(kernel, n_loc, n_tm), out_shape=(pltpu.V...]
where the time goes in v3:
time: 39.2 us; the launch traced here: 39 us
  Pallas kernels  37.1 us (95%)
  local copies, waits for them, and re-layouts  1.26 us (3%)
  between operations  0.64 us (2%)
    pallas_call x1, Pallas kernels, on_device(): pl.pallas_call(functools.partial(kernel, n_loc, n_tm), out_shape=(pltpu.V...  37.1 us
    unnamed x2, local copies, waits for them, and re-layouts  1.26 us

profile of v3, /device:TPU:0, one launch (start us, length us, event | category | flops | bytes accessed | tf_op | source)
XLA Modules:
  0.0 39.0 jit_solution(4488688406287853135)
XLA Ops:
  0.6 37.1 %shard_map.86 = (f32[128,128]{1,0:T(8,128)S(1)}, f32[128,128]{1,0:T(8,128)S(1)}) custom-call(f32[128,128]{1,0:T(8,128)} %obs_hbm.1, s32[128,128]{1,0:T(8,128)} %mask_hbm.1, f32[2,1024]{1,0:T(2,128)} %pos_hbm.1, f32[1,512]{1,0:T(1,128)} %bitcast.4, f32[1,128]{1,0:T(1,128)} %bitcast.5, f32[2,1024]{1,0:T(2,128)} %test_hbm.1, s32[1,1024]{1,0:T(1,128)} %bitcast.3), custom_call_target="tpu_custom_call" | custom-call | tf_op jit(solution)/shard_map/pallas_call | solution.py:309
  37.8 0.6 %copy.11 = f32[128,128]{1,0:T(8,128)} copy(f32[128,128]{1,0:T(8,128)S(1)} %get-tuple-element.2) | data formatting | bytes 131072
  38.4 0.6 %copy.12 = f32[128,128]{1,0:T(8,128)} copy(f32[128,128]{1,0:T(8,128)S(1)} %get-tuple-element.3) | data formatting | bytes 131072
